TPU v7x, 32 devices: a whole 2x2x4 slice. The times are simulated.
32 devices in a mesh: section: 2 (over y), dp: 16 (over z, x, core).
Axes of the slice: x: 2, y: 2, z: 4, core: 2. Of those that a mesh axis runs over, the one named last changes fastest.
Arguments:
- chars: bfloat16 [8192, 16, 256], P('dp'), may hold values from -6 to 6
- char_lengths: int32 [8192], P('dp'), may hold values from 1 to 16, as said below
- word_mask: int32 [8192], P('dp'), may hold values from 0 to 1, as said below
- out_grad: bfloat16 [8192, 512], P('dp'), may hold values from -6 to 6
- char_gain_a: bfloat16 [256], replicated, may hold values from 0.5 to 1.5
- char_qkv: bfloat16 [256, 768], replicated, may hold values from -0.375 to 0.375
- char_out: bfloat16 [256, 256], replicated, may hold values from -0.75 to 0.75
- char_gain_b: bfloat16 [256], replicated, may hold values from 0.5 to 1.5
- char_up: bfloat16 [256, 1024], replicated, may hold values from -0.375 to 0.375
- char_down: bfloat16 [1024, 256], replicated, may hold values from -0.25 to 0.25
- pool_gain: bfloat16 [256], replicated, may hold values from 0.5 to 1.5
- pool_query: bfloat16 [256], replicated, may hold values from -12 to 12
- char_proj: bfloat16 [256, 512], replicated, may hold values from -0.375 to 0.375
- word_gain_a: bfloat16 [512], replicated, may hold values from 0.5 to 1.5
- word_qkv: bfloat16 [512, 1536], replicated, may hold values from -0.25 to 0.25
- word_out: bfloat16 [512, 512], replicated, may hold values from -1.5 to 1.5
- word_gain_b: bfloat16 [512], replicated, may hold values from 0.5 to 1.5
- word_up: bfloat16 [512, 2048], replicated, may hold values from -0.25 to 0.25
- word_down: bfloat16 [2048, 512], replicated, may hold values from -0.1875 to 0.1875
Outputs:
- word_outputs: bfloat16 [8192, 512], P('dp', 'section')
- char_grad: bfloat16 [8192, 16, 256], P('dp', None, 'section')
- char_gain_a_grad: float32 [256], replicated
- char_qkv_grad: float32 [256, 768], replicated
- char_out_grad: float32 [256, 256], replicated
- char_gain_b_grad: float32 [256], replicated
- char_up_grad: float32 [256, 1024], replicated
- char_down_grad: float32 [1024, 256], replicated
- pool_gain_grad: float32 [256], replicated
- pool_query_grad: float32 [256], replicated
- char_proj_grad: float32 [256, 512], replicated
- word_gain_a_grad: float32 [512], replicated
- word_qkv_grad: float32 [512, 1536], replicated
- word_out_grad: float32 [512, 512], replicated
- word_gain_b_grad: float32 [512], replicated
- word_up_grad: float32 [512, 2048], replicated
- word_down_grad: float32 [2048, 512], replicated
Inputs may be any that keep to these rules, and one draw needn't show every extreme that they name: `char_lengths`: every word has at least one character; some word has all 16. `word_mask`: within each sequence the ones form a prefix that starts at its first word and covers at least half of it; at least one sequence has no padding.
All inputs are finite; a program needn't handle non-finite values.
Results may differ from a plain program's by a relative error of at most 0.023.
Values may be sent and summed in bfloat16 or wider, within the bound.
No kernel may reach another device: no remote copies, remote signals or barrier semaphores. Data moves between devices by JAX's collectives and lax.ppermute only.
A program may use at most 256 MiB of HBM per device.

v0:
```python
import jax
import jax.numpy as jnp
from jax import lax
from jax.sharding import PartitionSpec as P

CHEADS = 4
WHEADS = 8
MICRO = 2


EPSILON = 1e-06
NEGATIVE = -1e30


def swapped(value, axis, bit):
    mask = 2**bit
    pairs = [(source, source ^ mask) for source in range(lax.axis_size(axis))]
    return lax.ppermute(value, axis, pairs)


def rounded(value):
    return value.astype(jnp.bfloat16)


def product(left, right):
    return jnp.dot(left, right, preferred_element_type=jnp.float32)


def back_product(grad, weight):
    return lax.dot_general(
        grad, weight, (((grad.ndim - 1,), (1,)), ((), ())), preferred_element_type=jnp.float32
    )


def weight_grad(inputs, grad):
    flat_in = inputs.reshape(-1, inputs.shape[-1])
    flat_grad = grad.reshape(-1, grad.shape[-1])
    return lax.dot_general(
        flat_in, flat_grad, (((0,), (0,)), ((), ())), preferred_element_type=jnp.float32
    )


def rms_scale(value, gain):
    return value * lax.rsqrt(jnp.mean(value * value, axis=-1, keepdims=True) + EPSILON) * gain


def pool_words(states, gain, query, valid):
    normed = rms_scale(states, gain)
    score = jnp.sum(normed * query, axis=-1) * states.shape[-1] ** (-0.5)
    score = jnp.where(valid, score, NEGATIVE)
    weights = jax.nn.softmax(score, axis=-1)
    return jnp.sum(weights[..., None] * normed, axis=-2)


def gelu_grad(pre_act, grad):
    return jax.vjp(jax.nn.gelu, pre_act)[1](grad)[0]


def norm_grad(value, gain, grad):
    return jax.vjp(rms_scale, value, gain)[1](grad)


def softmax_grad(probs, grad):
    return probs * (grad - jnp.sum(grad * probs, axis=-1, keepdims=True))


def char_forward(chars, lens, weights):
    gain_a, w_qkv, w_out, gain_b, w_up, w_down, gain_p, query_p, w_proj = weights
    words, count, width = chars.shape
    size = width // CHEADS
    scale = size ** (-0.5)
    inputs = chars.astype(jnp.float32)
    valid = lax.broadcasted_iota(jnp.int32, (words, count), 1) < lens[:, None]
    low_a = rounded(rms_scale(inputs, gain_a.astype(jnp.float32)))
    qkv = rounded(product(low_a, w_qkv)).reshape(words, count, 3, CHEADS, size)
    query, keys, values = (qkv[:, :, 0], qkv[:, :, 1], qkv[:, :, 2])
    score = jnp.einsum("wqhd,wkhd->whqk", query, keys, preferred_element_type=jnp.float32) * scale
    score = jnp.where(valid[:, None, None, :], score, NEGATIVE)
    probs = jax.nn.softmax(score, axis=-1)
    probs_low = rounded(probs)
    mixed = jnp.einsum("whqk,wkhd->wqhd", probs_low, values, preferred_element_type=jnp.float32)
    mixed = rounded(mixed.reshape(words, count, width))
    after_a = inputs + product(mixed, w_out)
    low_b = rounded(rms_scale(after_a, gain_b.astype(jnp.float32)))
    pre_act = product(low_b, w_up)
    hidden = rounded(jax.nn.gelu(pre_act))
    after_b = after_a + product(hidden, w_down)
    pooled = rounded(
        pool_words(after_b, gain_p.astype(jnp.float32), query_p.astype(jnp.float32), valid)
    )
    vector = rounded(product(pooled, w_proj))
    saved = (
        inputs,
        valid,
        low_a,
        query,
        keys,
        values,
        probs,
        probs_low,
        mixed,
        after_a,
        low_b,
        pre_act,
        hidden,
        after_b,
        pooled,
    )
    return (vector, saved)


def char_backward(chars, lens, weights, grad_vec):
    gain_a, w_qkv, w_out, gain_b, w_up, w_down, gain_p, query_p, w_proj = weights
    saved = char_forward(chars, lens, weights)[1]
    (
        inputs,
        valid,
        low_a,
        query,
        keys,
        values,
        probs,
        probs_low,
        mixed,
        after_a,
        low_b,
        pre_act,
        hidden,
        after_b,
        pooled,
    ) = saved
    words, count, width = chars.shape
    scale = (width // CHEADS) ** (-0.5)
    d_proj = weight_grad(pooled, grad_vec)
    d_pooled = back_product(grad_vec, w_proj)
    pool_pull = jax.vjp(
        lambda states, gain, query_vec: pool_words(states, gain, query_vec, valid),
        after_b,
        gain_p.astype(jnp.float32),
        query_p.astype(jnp.float32),
    )[1]
    d_after_b, d_gain_p, d_query_p = pool_pull(d_pooled)
    branch = rounded(d_after_b)
    d_down = weight_grad(hidden, branch)
    d_pre = rounded(gelu_grad(pre_act, back_product(branch, w_down)))
    d_up = weight_grad(low_b, d_pre)
    d_norm_b, d_gain_b = norm_grad(after_a, gain_b.astype(jnp.float32), back_product(d_pre, w_up))
    d_after_a = d_after_b + d_norm_b
    branch_a = rounded(d_after_a)
    d_out = weight_grad(mixed, branch_a)
    d_mixed = rounded(back_product(branch_a, w_out)).reshape(words, count, CHEADS, -1)
    d_probs = jnp.einsum("wqhd,wkhd->whqk", d_mixed, values, preferred_element_type=jnp.float32)
    d_values = jnp.einsum("whqk,wqhd->wkhd", probs_low, d_mixed, preferred_element_type=jnp.float32)
    d_score = rounded(softmax_grad(probs, d_probs))
    d_query = (
        jnp.einsum("whqk,wkhd->wqhd", d_score, keys, preferred_element_type=jnp.float32) * scale
    )
    d_keys = (
        jnp.einsum("whqk,wqhd->wkhd", d_score, query, preferred_element_type=jnp.float32) * scale
    )
    d_qkv = rounded(jnp.stack([d_query, d_keys, d_values], axis=2).reshape(words, count, 3 * width))
    d_qkv_w = weight_grad(low_a, d_qkv)
    d_norm_a, d_gain_a = norm_grad(inputs, gain_a.astype(jnp.float32), back_product(d_qkv, w_qkv))
    d_chars = rounded(d_after_a + d_norm_a)
    return (
        d_chars,
        (d_gain_a, d_qkv_w, d_out, d_gain_b, d_up, d_down, d_gain_p, d_query_p, d_proj),
    )


def word_pass(vector, grad_out, weights, own_mask):
    gain_c, w_qkv, w_out, gain_d, w_up, w_down = weights
    rows, width = vector.shape
    size = width // WHEADS
    scale = size ** (-0.5)
    inputs = vector.astype(jnp.float32)
    low_c = rounded(rms_scale(inputs, gain_c.astype(jnp.float32)))
    qkv = rounded(product(low_c, w_qkv))
    query_pos = lax.broadcasted_iota(jnp.int32, (rows, rows), 0)
    key_pos = lax.broadcasted_iota(jnp.int32, (rows, rows), 1)
    allowed = (key_pos <= query_pos) & (own_mask > 0)[None, :]
    query = qkv[:, :width].reshape(rows, WHEADS, size)
    keys = qkv[:, width : 2 * width].reshape(rows, WHEADS, size)
    values = qkv[:, 2 * width :].reshape(rows, WHEADS, size)
    score = jnp.einsum("qhd,khd->hqk", query, keys, preferred_element_type=jnp.float32) * scale
    score = jnp.where(allowed[None], score, NEGATIVE)
    probs = jax.nn.softmax(score, axis=-1)
    probs_low = rounded(probs)
    mixed = rounded(
        jnp.einsum("hqk,khd->qhd", probs_low, values, preferred_element_type=jnp.float32).reshape(
            rows, width
        )
    )
    after_a = inputs + product(mixed, w_out)
    low_d = rounded(rms_scale(after_a, gain_d.astype(jnp.float32)))
    pre_act = product(low_d, w_up)
    hidden = rounded(jax.nn.gelu(pre_act))
    result = rounded(after_a + product(hidden, w_down))
    d_down = weight_grad(hidden, grad_out)
    d_pre = rounded(gelu_grad(pre_act, back_product(grad_out, w_down)))
    d_up = weight_grad(low_d, d_pre)
    d_norm_d, d_gain_d = norm_grad(after_a, gain_d.astype(jnp.float32), back_product(d_pre, w_up))
    d_after_a = grad_out.astype(jnp.float32) + d_norm_d
    branch_a = rounded(d_after_a)
    d_out = weight_grad(mixed, branch_a)
    d_mixed = rounded(back_product(branch_a, w_out)).reshape(rows, WHEADS, size)
    d_probs = jnp.einsum("qhd,khd->hqk", d_mixed, values, preferred_element_type=jnp.float32)
    d_values = jnp.einsum("hqk,qhd->khd", probs_low, d_mixed, preferred_element_type=jnp.float32)
    d_score = rounded(softmax_grad(probs, d_probs))
    d_query = jnp.einsum("hqk,khd->qhd", d_score, keys, preferred_element_type=jnp.float32) * scale
    d_keys = jnp.einsum("hqk,qhd->khd", d_score, query, preferred_element_type=jnp.float32) * scale
    d_qkv = rounded(
        jnp.concatenate(
            [
                d_query.reshape(rows, width),
                d_keys.reshape(rows, width),
                d_values.reshape(rows, width),
            ],
            axis=1,
        )
    )
    d_qkv_w = weight_grad(low_c, d_qkv)
    d_norm_c, d_gain_c = norm_grad(inputs, gain_c.astype(jnp.float32), back_product(d_qkv, w_qkv))
    d_vec = rounded(d_after_a + d_norm_c)
    return (result, d_vec, (d_gain_c, d_qkv_w, d_out, d_gain_d, d_up, d_down))


def cross_section(buffer):
    return swapped(buffer, "section", 0)


def word_round(is_char, vector, mask_piece, grad_piece, weights):
    rows, width = vector.shape
    blank = (
        jnp.zeros((rows, width), jnp.bfloat16),
        jnp.zeros((rows, width), jnp.bfloat16),
        tuple((jnp.zeros(w.shape, jnp.float32) for w in weights)),
    )
    return lax.cond(
        is_char, lambda: blank, lambda: word_pass(vector, grad_piece, weights, mask_piece)
    )


def body(
    chars,
    char_lengths,
    word_mask,
    out_grad,
    char_gain_a,
    char_qkv,
    char_out,
    char_gain_b,
    char_up,
    char_down,
    pool_gain,
    pool_query,
    char_proj,
    word_gain_a,
    word_qkv,
    word_out,
    word_gain_b,
    word_up,
    word_down,
):
    char_weights = (
        char_gain_a,
        char_qkv,
        char_out,
        char_gain_b,
        char_up,
        char_down,
        pool_gain,
        pool_query,
        char_proj,
    )
    word_weights = (word_gain_a, word_qkv, word_out, word_gain_b, word_up, word_down)
    is_char = lax.axis_index("section") == 0
    rows = chars.shape[0] // MICRO
    width = word_qkv.shape[0]

    def piece(array, index):
        return array[index * rows : (index + 1) * rows]

    blank_vec = jnp.zeros((rows, width), jnp.bfloat16)
    blank_chars = jnp.zeros((rows,) + chars.shape[1:], jnp.bfloat16)
    char_grads = tuple((jnp.zeros(w.shape, jnp.float32) for w in char_weights))
    word_grads = tuple((jnp.zeros(w.shape, jnp.float32) for w in word_weights))
    word_pieces = []
    char_pieces = []
    received = blank_vec
    for tick in range(MICRO + 2):
        if tick >= 2:
            index = tick - 2
            d_piece, grads = lax.cond(
                is_char,
                lambda: char_backward(
                    piece(chars, index), piece(char_lengths, index), char_weights, received
                ),
                lambda: (
                    blank_chars,
                    tuple((jnp.zeros(w.shape, jnp.float32) for w in char_weights)),
                ),
            )
            char_pieces.append(d_piece)
            char_grads = tuple((a + b for a, b in zip(char_grads, grads)))
        send = blank_vec
        if tick < MICRO:
            send = lax.cond(
                is_char,
                lambda: char_forward(piece(chars, tick), piece(char_lengths, tick), char_weights)[
                    0
                ],
                lambda: blank_vec,
            )
        if 1 <= tick <= MICRO:
            index = tick - 1
            result, d_vec, grads = word_round(
                is_char, received, piece(word_mask, index), piece(out_grad, index), word_weights
            )
            word_pieces.append(result)
            word_grads = tuple((a + b for a, b in zip(word_grads, grads)))
            send = jnp.where(is_char, send, d_vec)
        if tick <= MICRO:
            received = cross_section(send)
    word_full = jnp.concatenate(word_pieces, axis=0)
    chars_full = jnp.concatenate(char_pieces, axis=0)
    word_half = width // 2
    char_half = chars.shape[2] // 2
    theirs = swapped((word_full[:, :word_half], chars_full[:, :, char_half:]), "section", 0)
    word_outputs = jnp.where(is_char, theirs[0], word_full[:, word_half:])
    char_grad = jnp.where(is_char, chars_full[:, :, :char_half], theirs[1])
    summed = lax.psum(char_grads + word_grads, ("section", "dp"))
    return (word_outputs, char_grad) + tuple(summed)


def solution(mesh):
    return jax.shard_map(
        body,
        mesh=mesh,
        in_specs=(
            P("dp", None, None),
            P("dp"),
            P("dp"),
            P("dp", None),
            P(),
            P(),
            P(),
            P(),
            P(),
            P(),
            P(),
            P(),
            P(),
            P(),
            P(),
            P(),
            P(),
            P(),
            P(),
        ),
        out_specs=(
            P("dp", "section"),
            P("dp", None, "section"),
            P(),
            P(),
            P(),
            P(),
            P(),
            P(),
            P(),
            P(),
            P(),
            P(),
            P(),
            P(),
            P(),
            P(),
            P(),
        ),
        check_vma=False,
    )
```

profile of v0, /device:TPU:1, one launch (start us, length us, event | category | flops | bytes accessed | tf_op | source)
XLA Modules:
  0.0 1122.9 jit_solution(8541217076362138835)
XLA Ops:
  7.2 111.6 %conditional.6 = (bf16[256,512]{1,0:T(8,128)(2,1)S(1)}) conditional(s32[]{:T(128)} %convert_element_type.348, () %tuple.52, (s32[512]{0:T(512)}, bf16[512,16,256]{2,1,0:T(8,128)(2,1)}, bf16[256]{0:T(256)(128)(2,1)}, bf16[256,768]{1,0:T(8,128)(2,1)}, bf16[256,256]{1,0:T(8,128)(2,1)}, /*index=5*/bf16[256]{0:T(256)(128)(2,1)}, ...), branch_computations={%region_0.0_spmd, %region_1.11_spmd} | conditional | flops 6646535168 | bytes 129710272 | solution.py:308
  10.6 7.5 copy.430
  26.4 8.6 copy.339
  40.8 7.4 copy.506
  48.3 7.4 copy.505
  62.3 9.0 fusion.12
  85.2 7.7 convert_bitcast_fusion
  102.5 11.7 %multiply_reduce_fusion.2 = (f32[256,16]{0,1:T(8,128)S(1)}, f32[256,16,256]{0,2,1:T(8,128)}) fusion(f32[256,16,256]{0,2,1:T(8,128)} %get-tuple-element.526, bf16[1024,256]{1,0:T(8,128)(2,1)S(1)} %copy-done.114, f32[256]{0:T(256)S(1)} %convert_element_type.247, f32[256,16]{0,1:T(8,128)S(1)} %add_rsqrt_fusion.1, bf16[256,1024]{1,0:T(8,128)(2,1)S(1)} %copy-done.49), kind=kOutput, calls=%fused_computation.24 | convolution fusion | flops 4339003392 | bytes 9470976 | tf_op jit(solution)/shard_map/cond/branch_1_fun/dot_general | solution.py:26
  119.5 111.7 %conditional.8 = (bf16[256,512]{1,0:T(8,128)(2,1)S(1)}) conditional(s32[]{:T(128)} %convert_element_type.348, () %tuple.56, (s32[512]{0:T(512)}, bf16[512,16,256]{2,1,0:T(8,128)(2,1)}, bf16[256]{0:T(256)(128)(2,1)}, bf16[256,768]{1,0:T(8,128)(2,1)}, bf16[256,256]{1,0:T(8,128)(2,1)}, /*index=5*/bf16[256]{0:T(256)(128)(2,1)}, ...), branch_computations={%region_22.23_spmd, %region_23.33_spmd} | conditional | flops 6646535168 | bytes 125515904 | solution.py:308
  122.9 7.5 copy.433
  138.8 8.6 copy.357
  153.2 7.4 copy.509
  160.6 7.4 copy.508
  174.7 9.0 fusion.112
  197.8 7.7 convert_bitcast_fusion.1
  215.0 11.7 %multiply_reduce_fusion.10 = (f32[256,16]{0,1:T(8,128)S(1)}, f32[256,16,256]{0,2,1:T(8,128)}) fusion(f32[256,16,256]{0,2,1:T(8,128)} %get-tuple-element.546, bf16[1024,256]{1,0:T(8,128)(2,1)} %get-tuple-element.447, f32[256]{0:T(256)S(1)} %convert_element_type.280, f32[256,16]{0,1:T(8,128)S(1)} %add_rsqrt_fusion.4, bf16[256,1024]{1,0:T(8,128)(2,1)} %get-tuple-element.164), kind=kOutput, calls=%fused_computation.167 | convolution fusion | flops 4339003392 | bytes 9470976 | tf_op jit(solution)/shard_map/cond/branch_1_fun/dot_general | solution.py:26
  231.9 8.0 conditional.7
  241.2 7.9 collective-permute-done.1
  249.0 9.0 conditional.9
  258.8 24.0 %collective-permute-start.3 = (bf16[256,512]{1,0:T(8,128)(2,1)}, bf16[256,512]{1,0:T(8,128)(2,1)}, u32[]{:S(2)}, u32[]{:S(2)}) collective-permute-start(bf16[256,512]{1,0:T(8,128)(2,1)} %broadcast_select_fusion), channel_id=1, source_target_pairs={{0,16},{16,0},{1,17},{17,1},{2,18},{18,2},{3,19},{19,3},{4,20},{20... | collective-permute-start | bytes 786440 | tf_op jit(solution)/shard_map/ppermute | solution.py:18
  282.7 247.8 %conditional.10 = (f32[256]{0:T(256)}, f32[256,768]{1,0:T(8,128)}, f32[256,256]{1,0:T(8,128)}, f32[256]{0:T(256)}, f32[256,1024]{1,0:T(8,128)}, /*index=5*/f32[1...) conditional(s32[]{:T(128)} %convert_element_type.348, () %tuple.59, ...), branch_computations={%region_44.45_spmd, %region_45.65_spmd} | conditional | flops 19947417600 | bytes 510288640 | solution.py:294
  287.4 7.7 copy.436
  303.5 8.7 copy.375
  318.0 7.5 copy.511
  325.5 7.5 copy.510
  345.4 28.7 %fusion.353 = (f32[256,4,16]{2,1,0:T(4,128)S(1)}, f32[256,4,16,16]{2,3,1,0:T(8,128)S(1)}) fusion(f32[256,4,16,16]{2,3,1,0:T(8,128)S(1)} %fusion.222, pred[256,16]{1,0:T(8,128)(4,1)S(1)} %copy.377), kind=kOutput, calls=%fused_computation.531 | output fusion | flops 1572879 | bytes 2166784 | tf_op jit(solution)/shard_map/cond/branch_1_fun/sub | solution.py:79
  388.3 8.2 fusion.250
  396.5 9.6 multiply_reduce_fusion.25
  411.5 11.0 convolution_bitcast_fusion
  422.4 18.2 %fusion.207 = bf16[256,16,1024]{2,0,1:T(8,128)(2,1)} fusion(f32[256,16,1024]{2,0,1:T(8,128)} %fusion.250, bf16[1024,256]{1,0:T(8,128)(2,1)S(1)} %copy-done.115, f32[256,16,256]{0,2,1:T(8,128)S(1)} %get-tuple-element.570, f32[256,16]{0,1:T(8,128)S(1)} %multiply_multiply_fusion.17, f32[256,16]{0,1:T(8,128)S(1)} %get-tuple-element.564, ...), kind=kOutput, calls=%fused_computation.295 | convolution fusion | flops 2240806912 | bytes 30214144 | tf_op jit(solution)/shard_map/cond/branch_1_fun/dot_general | solution.py:30
  463.1 9.0 convert_bitcast_fusion.2
  472.2 10.6 multiply_reduce_fusion.16
  501.0 15.4 %copy.393 = bf16[256,16,3,4,64]{0,4,3,2,1:T(8,128)(2,1)} copy(bf16[256,16,3,4,64]{4,1,3,0,2:T(8,128)(2,1)} %pad_maximum_fusion.6) | data formatting | bytes 12582912 | tf_op jit(solution)/shard_map/cond/branch_1_fun/stack | solution.py:161
  550.3 245.8 %conditional.11 = (f32[256]{0:T(256)}, f32[256,768]{1,0:T(8,128)}, f32[256,256]{1,0:T(8,128)}, f32[256]{0:T(256)}, f32[256,1024]{1,0:T(8,128)}, /*index=5*/f32[1...) conditional(s32[]{:T(128)} %convert_element_type.348, () %tuple.61, ...), branch_computations={%region_65.66_spmd, %region_66.86_spmd} | conditional | flops 19947417600 | bytes 508191488 | solution.py:294
  552.2 7.5 copy.437
  568.0 8.7 copy.403
  582.4 7.5 copy.514
  589.9 7.5 copy.513
  609.9 28.7 %fusion.355 = (f32[256,4,16]{2,1,0:T(4,128)S(1)}, f32[256,4,16,16]{2,3,1,0:T(8,128)S(1)}) fusion(f32[256,4,16,16]{2,3,1,0:T(8,128)S(1)} %fusion.292, pred[256,16]{1,0:T(8,128)(4,1)S(1)} %copy.405), kind=kOutput, calls=%fused_computation.533 | output fusion | flops 1572879 | bytes 2166784 | tf_op jit(solution)/shard_map/cond/branch_1_fun/sub | solution.py:79
  652.7 8.2 fusion.320
  660.8 9.6 multiply_reduce_fusion.37
  676.8 11.0 convolution_bitcast_fusion.4
  687.8 18.0 %fusion.277 = bf16[256,16,1024]{2,0,1:T(8,128)(2,1)} fusion(f32[256,16,1024]{2,0,1:T(8,128)} %fusion.320, bf16[1024,256]{1,0:T(8,128)(2,1)S(1)} %copy-done.116, f32[256,16,256]{0,2,1:T(8,128)S(1)} %get-tuple-element.585, f32[256,16]{0,1:T(8,128)S(1)} %multiply_multiply_fusion.23, f32[256,16]{0,1:T(8,128)S(1)} %get-tuple-element.579, ...), kind=kOutput, calls=%fused_computation.409 | convolution fusion | flops 2240806912 | bytes 30214144 | tf_op jit(solution)/shard_map/cond/branch_1_fun/dot_general | solution.py:30
  728.6 9.0 convert_bitcast_fusion.4
  737.6 10.5 multiply_reduce_fusion.28
  766.6 15.3 %copy.421 = bf16[256,16,3,4,64]{0,4,3,2,1:T(8,128)(2,1)} copy(bf16[256,16,3,4,64]{4,1,3,0,2:T(8,128)(2,1)} %pad_maximum_fusion.7) | data formatting | bytes 12582912 | tf_op jit(solution)/shard_map/cond/branch_1_fun/stack | solution.py:161
  819.3 116.3 %all-reduce = (f32[256]{0:T(256)}, f32[256]{0:T(256)}, f32[256]{0:T(256)}, f32[256]{0:T(256)}, f32[512]{0:T(512)}, /*index=5*/f32[512]{0:T(512)}) all-reduce(f32[256]{0:T(256)S(1)} %add.341, f32[256]{0:T(256)S(1)} %add.344, f32[256]{0:T(256)S(1)} %add.347, f32[256]{0:T(256)S(1)} %add.348, ...), channel_id=1, replica_groups=mesh['section'=2,'dp'=16] {'section','dp'}, use_global_device_ids=true, to_apply=%region_86.87 | all-reduce | flops 2048 | bytes 16384 | tf_op jit(solution)/shard_map/psum | solution.py:332
  939.5 158.9 %all-reduce.4.cloned.1.call-done = (f32[256,768]{1,0:T(8,128)}, f32[256,256]{1,0:T(8,128)}, f32[256,1024]{1,0:T(8,128)}, f32[1024,256]{1,0:T(8,128)}, f32[256,51...) async-done(((f32[256,768]{1,0:T(8,128)}, f32[256,256]{1,0:T(8,128)}, f32[256,1024]{1,0:T(8,128)}, ...) | async-done | bytes 16252944 | tf_op jit(solution)/shard_map/psum | solution.py:332
  (380 shorter events, 395.9 us)
Async XLA Ops:
  7.2 1091.3 %all-reduce.4.cloned.1.call-start = ((), (), s32[]{:S(2)}) async-start(), calls=%async_computation | async-start | bytes 32505856 | tf_op jit(solution)/shard_map/psum | solution.py:332
  10.6 9.6 copy-start.118
  119.5 111.7 %collective-permute-start = (bf16[256,512]{1,0:T(8,128)(2,1)}, bf16[256,512]{1,0:T(8,128)(2,1)S(1)}, u32[]{:S(2)}, u32[]{:S(2)}) collective-permute-start(bf16[256,512]{1,0:T(8,128)(2,1)} %copy-done.85), channel_id=1, source_target_pairs={{0,16},{16,0},{1,17},{17,1},{2,18},{18,2},{3,19},{19,3},{4,20},{20... | collective-permute-start | bytes 786440 | tf_op jit(solution)/shard_map/ppermute | solution.py:18
  119.5 111.7 %copy-start.17 = (bf16[512,512]{1,0:T(8,128)(2,1)S(1)}, bf16[512,512]{1,0:T(8,128)(2,1)}, u32[]{:S(2)}) copy-start(bf16[512,512]{1,0:T(8,128)(2,1)} %param.46) | copy-start | bytes 1572868
  119.5 111.7 %copy-start.99 = (bf16[512]{0:T(512)(128)(2,1)S(1)}, bf16[512]{0:T(512)(128)(2,1)}, u32[]{:S(2)}) copy-start(bf16[512]{0:T(512)(128)(2,1)} %param.44) | copy-start | bytes 3076
  119.5 111.7 %copy-start.100 = (bf16[512]{0:T(512)(128)(2,1)S(1)}, bf16[512]{0:T(512)(128)(2,1)}, u32[]{:S(2)}) copy-start(bf16[512]{0:T(512)(128)(2,1)} %param.47) | copy-start | bytes 3076
  119.5 111.7 %copy-start.124 = (s32[512]{0:T(512)S(1)}, s32[512]{0:T(512)}, u32[]{:S(2)}) copy-start(s32[512]{0:T(512)} %param.33) | copy-start | bytes 6148
  122.9 9.6 copy-start.119
  239.9 9.1 copy-start.28
  239.9 9.1 copy-start.101
  239.9 9.1 copy-start.104
  241.1 7.9 collective-permute-start.1
  249.0 33.7 %copy-start.25 = (bf16[256,256]{1,0:T(8,128)(2,1)S(1)}, bf16[256,256]{1,0:T(8,128)(2,1)}, u32[]{:S(2)}) copy-start(bf16[256,256]{1,0:T(8,128)(2,1)} %param.37) | copy-start | bytes 393220
  258.0 24.7 %copy-start.30 = (f32[512,512]{1,0:T(8,128)}, f32[512,512]{1,0:T(8,128)S(1)}, u32[]{:S(2)}) copy-start(f32[512,512]{1,0:T(8,128)S(1)} %get-tuple-element.284) | copy-start | bytes 3145732
  258.0 24.7 %copy-start.106 = (f32[512]{0:T(512)}, f32[512]{0:T(512)S(1)}, u32[]{:S(2)}) copy-start(f32[512]{0:T(512)S(1)} %get-tuple-element.280) | copy-start | bytes 6148
  258.8 291.4 %collective-permute-start.3 = (bf16[256,512]{1,0:T(8,128)(2,1)}, bf16[256,512]{1,0:T(8,128)(2,1)}, u32[]{:S(2)}, u32[]{:S(2)}) collective-permute-start(bf16[256,512]{1,0:T(8,128)(2,1)} %broadcast_select_fusion), channel_id=1, source_target_pairs={{0,16},{16,0},{1,17},{17,1},{2,18},{18,2},{3,19},{19,3},{4,20},{20... | collective-permute-start | bytes 786440 | tf_op jit(solution)/shard_map/ppermute | solution.py:18
  286.1 11.2 copy-start.108
  287.4 9.8 copy-start.120
  345.4 32.0 %copy-start.35 = (bf16[256,16,1,4,64]{4,1,3,0,2:T(8,128)(2,1)S(1)}, bf16[256,16,1,4,64]{4,1,3,0,2:T(8,128)(2,1)}, u32[]{:S(2)}) copy-start(bf16[256,16,1,4,64]{4,1,3,0,2:T(8,128)(2,1)} %copy.512) | copy-start | bytes 6291460 | tf_op jit(solution)/shard_map/cond
  388.3 8.2 copy-start.115
  440.6 6.9 copy-start.129
  456.3 6.8 copy-start.75
  463.1 9.0 copy-start.36
  482.7 7.3 copy-start.4
  501.0 15.4 %copy-start.91 = (f32[256,16]{0,1:T(8,128)S(1)}, f32[256,16]{0,1:T(8,128)}, u32[]{:S(2)}) copy-start(f32[256,16]{0,1:T(8,128)} %copy-done.90) | copy-start | bytes 49156 | tf_op jit(solution)/shard_map/cond
  501.0 15.4 %copy-start.109 = (f32[256]{0:T(256)S(1)}, f32[256]{0:T(256)}, u32[]{:S(2)}) copy-start(f32[256]{0:T(256)} %copy-done.108) | copy-start | bytes 3076 | tf_op jit(solution)/shard_map/cond
  516.4 6.7 copy-start.121
  537.1 6.7 copy-start.29
  537.1 6.7 copy-start.31
  550.7 11.0 copy-start.122
  550.8 10.9 copy-start.110
  609.9 32.1 %copy-start.37 = (bf16[256,16,1,4,64]{4,1,3,0,2:T(8,128)(2,1)S(1)}, bf16[256,16,1,4,64]{4,1,3,0,2:T(8,128)(2,1)}, u32[]{:S(2)}) copy-start(bf16[256,16,1,4,64]{4,1,3,0,2:T(8,128)(2,1)} %copy.515) | copy-start | bytes 6291460 | tf_op jit(solution)/shard_map/cond
  652.6 8.2 copy-start.116
  705.8 6.9 copy-start.130
  721.6 7.0 copy-start.77
  728.6 9.0 copy-start.38
  748.2 7.4 copy-start.6
  766.6 15.3 %copy-start.93 = (f32[256,16]{0,1:T(8,128)S(1)}, f32[256,16]{0,1:T(8,128)}, u32[]{:S(2)}) copy-start(f32[256,16]{0,1:T(8,128)} %copy-done.92) | copy-start | bytes 49156 | tf_op jit(solution)/shard_map/cond
  766.6 15.4 %copy-start.111 = (f32[256]{0:T(256)S(1)}, f32[256]{0:T(256)}, u32[]{:S(2)}) copy-start(f32[256]{0:T(256)} %copy-done.110) | copy-start | bytes 3076 | tf_op jit(solution)/shard_map/cond
  782.0 6.7 copy-start.123
  809.4 7.1 copy-start.102
  809.4 7.1 copy-start.103
  809.4 7.1 copy-start.105
  809.4 7.1 copy-start.107
  814.9 121.5 %collective-permute-start.4 = (bf16[512,16,128]{2,1,0:T(8,128)(2,1)}, bf16[512,16,128]{2,1,0:T(8,128)(2,1)S(1)}, u32[]{:S(2)}, u32[]{:S(2)}) collective-permute-start(bf16[512,16,128]{2,1,0:T(8,128)(2,1)} %slice.135), channel_id=1, source_target_pairs={{0,16},{16,0},{1,17},{17,1},{2,18},{18,2},{3,19},{19,3},{4,20},{20... | collective-permute-start | bytes 6291464 | tf_op jit(solution)/shard_map/ppermute | solution.py:18
  815.0 120.7 %collective-permute-start.2 = (bf16[512,256]{1,0:T(8,128)(2,1)S(1)}, bf16[512,256]{1,0:T(8,128)(2,1)S(1)}, u32[]{:S(2)}, u32[]{:S(2)}) collective-permute-start(bf16[512,256]{1,0:T(8,128)(2,1)S(1)} %slice.132), channel_id=1, source_target_pairs={{0,16},{16,0},{1,17},{17,1},{2,18},{18,2},{3,19},{19,3},{4,20},{20... | collective-permute-start | bytes 786440 | tf_op jit(solution)/shard_map/ppermute | solution.py:18
  1098.5 7.2 copy-start.78
  1098.5 8.0 copy-start.43
  (48 other events, 202.8 us)
Sparse Core Ops, SparseCore 0:
  807.8 290.6 all-reduce.3
where the time goes:
time: 1140 us; the launch traced here: 1120 us
  local copies, waits for them, and re-layouts  326 us (29%)
  matrix products  305 us (27%)
  waiting for transfers between devices  167 us (15%)
  other arithmetic  166 us (15%)
  blocking collectives  116 us (10%)
  starting transfers between devices  25.6 us (2%)
  between operations  14.6 us (1%)
    psum x1, waiting for transfers between devices, body(): summed = lax.psum(char_grads + word_grads, ('section', 'dp'))  159 us
    psum x1, blocking collectives, body(): summed = lax.psum(char_grads + word_grads, ('section', 'dp'))  116 us
    dot_general x16, matrix products, product(): return jnp.dot(left, right, preferred_element_type=jnp.float32)  98.2 us
    cond x122, local copies, waits for them, and re-layouts  95.4 us
    convert_element_type x10, local copies, waits for them, and re-layouts, rounded(): return value.astype(jnp.bfloat16)  68.4 us
    sub x4, other arithmetic, char_forward(): probs = jax.nn.softmax(score, axis=-1)  58.4 us
    dot_general x10, matrix products, weight_grad(): lax.dot_general(flat_in, flat_grad, (((0,), (0,)), ((), ())), preferred_e...  55.3 us
    dot_general x10, matrix products, back_product(): lax.dot_general(grad, weight, (((grad.ndim - 1,), (1,)), ((), ())), prefe...  52.8 us
  transfers between devices with their start and end apart: 6, of which 2 were waited for; matrix products, arithmetic and copies ran while one was open for 34% of the time, Pallas kernels for 0%

commit v1 on v0

v1 whole, which is shorter than its diff:
```python
import functools

import jax
import jax.numpy as jnp
from jax import lax
from jax.experimental import pallas as pl
from jax.experimental.pallas import tpu as pltpu
from jax.sharding import PartitionSpec as P

CHEADS = 4
WHEADS = 8
EPSILON = 1e-06
NEGATIVE = -1e30
BLOCK_WORDS = 32
GROUP = 128
F32 = jnp.float32
BF16 = jnp.bfloat16
C0 = 0.7978845608028654
C1 = 0.7978845608028654 * 0.044715


def mm(left, right):
    return jnp.dot(left, right, preferred_element_type=F32)


def mm_nt(left, right):
    return lax.dot_general(left, right, (((1,), (1,)), ((), ())), preferred_element_type=F32)


def mm_tn(left, right):
    return lax.dot_general(left, right, (((0,), (0,)), ((), ())), preferred_element_type=F32)


def inverse_rms(value):
    return lax.rsqrt(jnp.mean(value * value, axis=-1, keepdims=True) + EPSILON)


def gelu(u):
    t = jnp.tanh(u * (C0 + C1 * (u * u)))
    half = 0.5 * u
    return half + half * t


def gelu_both(u):
    square = u * u
    t = jnp.tanh(u * (C0 + C1 * square))
    half = 0.5 * u
    slope = (0.5 + 0.5 * t) + half * (1.0 - t * t) * (C0 + (3.0 * C1) * square)
    return half + half * t, slope


def rms_back(unit, inverse, gain, grad):
    scaled = grad * gain
    d_value = inverse * (scaled - unit * jnp.mean(scaled * unit, axis=-1, keepdims=True))
    return d_value, jnp.sum(grad * unit, axis=0, keepdims=True)


def two_heads(pair):
    lane = lax.broadcasted_iota(jnp.int32, pair.shape, 1)
    zero = jnp.zeros_like(pair)
    return jnp.concatenate(
        [jnp.where(lane < 64, pair, zero), jnp.where(lane < 64, zero, pair)], axis=0
    )


def side(stacked):
    n = stacked.shape[0] // 2
    return jnp.concatenate([stacked[:n], stacked[n:]], axis=1)


def pool_forward(x2, gain, query, lens_rows):
    rows, width = x2.shape
    inverse = inverse_rms(x2)
    unit = x2 * inverse
    normed = unit * gain
    score = jnp.sum(normed * query, axis=-1, keepdims=True) * width ** (-0.5)
    words = rows // 16
    place = lax.broadcasted_iota(jnp.int32, (rows, 1), 0) % 16
    score = jnp.where(place < lens_rows, score, NEGATIVE)
    score = score.reshape(words, 16, 1)
    exps = jnp.exp(score - jnp.max(score, axis=1, keepdims=True))
    weights = exps / jnp.sum(exps, axis=1, keepdims=True)
    return inverse, unit, normed, weights


def lens_column(lens):
    row = lax.broadcasted_iota(jnp.int32, (GROUP, GROUP), 0)
    lane = lax.broadcasted_iota(jnp.int32, (GROUP, GROUP), 1)
    pick = row == lane
    out = []
    for g in range(lens.shape[0]):
        out.append(jnp.sum(jnp.where(pick, lens[g : g + 1], 0), axis=1, keepdims=True))
    return jnp.concatenate(out, axis=0)


def char_forward_kernel(
    sec_ref, chars, lens, gain_a, w_qkv, w_out, gain_b, w_up, w_down, gain_p, query_p, w_proj,
    qkv_out, o1_out, x1_out, u1_out, x2_out, pooled_out, e_out,
):
    words, slots, width = chars.shape
    rows = words * slots
    x = chars[...].reshape(rows, width).astype(F32)
    a1 = (x * inverse_rms(x) * gain_a[...].astype(F32)).astype(BF16)
    qkv_out[...] = mm(a1, w_qkv[...]).astype(BF16)
    row = lax.broadcasted_iota(jnp.int32, (GROUP, GROUP), 0)
    lane = lax.broadcasted_iota(jnp.int32, (GROUP, GROUP), 1)
    same = (row // 16) == (lane // 16)
    lens_now = lens[0]
    for g in range(rows // GROUP):
        at = slice(g * GROUP, (g + 1) * GROUP)
        allowed = same & ((lane % 16) < lens_now[g : g + 1])
        mask = jnp.where(allowed, 0.0, NEGATIVE)
        mask = jnp.concatenate([mask, mask], axis=0)
        for j in range(2):
            q = qkv_out[at, j * 128 : j * 128 + 128] * 0.125
            k = qkv_out[at, width + j * 128 : width + j * 128 + 128]
            v = qkv_out[at, 2 * width + j * 128 : 2 * width + j * 128 + 128]
            s = mm_nt(two_heads(q), k) + mask
            e = jnp.exp(s - jnp.max(s, axis=-1, keepdims=True))
            p = (e / jnp.sum(e, axis=-1, keepdims=True)).astype(BF16)
            o1_out[at, j * 128 : j * 128 + 128] = mm(side(p), two_heads(v)).astype(BF16)
    x1 = x + mm(o1_out[...], w_out[...])
    x1_out[...] = x1
    a2 = (x1 * inverse_rms(x1) * gain_b[...].astype(F32)).astype(BF16)
    u1 = mm(a2, w_up[...])
    u1_out[...] = u1.astype(BF16)
    h1 = gelu(u1).astype(BF16)
    x2 = x1 + mm(h1, w_down[...])
    x2_out[...] = x2
    _, _, normed, weights = pool_forward(
        x2, gain_p[...].astype(F32), query_p[...].astype(F32), lens_column(lens_now)
    )
    pooled = jnp.sum(weights * normed.reshape(words, 16, width), axis=1).astype(BF16)
    pooled_out[...] = pooled
    e_out[...] = mm(pooled, w_proj[...]).astype(BF16)


def word_kernel(
    e_ref, mask_ref, g_ref, pooled_ref, gain_c, w_qkv, w_out, gain_d, w_up, w_down, w_proj,
    out_ref, grads_ref, gains_ref, proj_ref, gpool_ref,
):
    rows, width = e_ref.shape
    hidden = w_up.shape[1]
    y = e_ref[...].astype(F32)
    gain_c_f = gain_c[...].astype(F32)
    gain_d_f = gain_d[...].astype(F32)
    inv_c = inverse_rms(y)
    unit_c = y * inv_c
    a3 = (unit_c * gain_c_f).astype(BF16)
    qkv = mm(a3, w_qkv[...]).astype(BF16)
    row = lax.broadcasted_iota(jnp.int32, (rows, rows), 0)
    lane = lax.broadcasted_iota(jnp.int32, (rows, rows), 1)
    allowed = (lane <= row) & (mask_ref[...] > 0)
    mask = jnp.where(allowed, 0.0, NEGATIVE)
    mask = jnp.concatenate([mask, mask], axis=0)
    pairs = width // 128
    probs, mixed = [], []
    for j in range(pairs):
        q = qkv[:, j * 128 : j * 128 + 128] * 0.125
        k = qkv[:, width + j * 128 : width + j * 128 + 128]
        v = qkv[:, 2 * width + j * 128 : 2 * width + j * 128 + 128]
        s = mm_nt(two_heads(q), k) + mask
        e = jnp.exp(s - jnp.max(s, axis=-1, keepdims=True))
        p = e / jnp.sum(e, axis=-1, keepdims=True)
        probs.append(p)
        mixed.append(mm(side(p.astype(BF16)), two_heads(v)).astype(BF16))
    o2 = jnp.concatenate(mixed, axis=1)
    y1 = y + mm(o2, w_out[...])
    inv_d = inverse_rms(y1)
    unit_d = y1 * inv_d
    a4 = (unit_d * gain_d_f).astype(BF16)
    u2 = mm(a4, w_up[...])
    h2, slope = gelu_both(u2)
    h2 = h2.astype(BF16)
    out_ref[...] = (y1 + mm(h2, w_down[...])).astype(BF16)
    g = g_ref[...]
    grads_ref[0:hidden, :] = mm_tn(h2, g).astype(BF16)
    g_u2 = (slope * mm_nt(g, w_down[...])).astype(BF16)
    at = hidden
    for j in range(hidden // width):
        grads_ref[at : at + width, :] = mm_tn(a4, g_u2[:, j * width : (j + 1) * width]).astype(BF16)
        at += width
    d_y1n, d_gain_d = rms_back(unit_d, inv_d, gain_d_f, mm_nt(g_u2, w_up[...]))
    g_y1 = g.astype(F32) + d_y1n
    g_b1 = g_y1.astype(BF16)
    grads_ref[at : at + width, :] = mm_tn(o2, g_b1).astype(BF16)
    at += width
    g_o2 = mm_nt(g_b1, w_out[...]).astype(BF16)
    d_q, d_k, d_v = [], [], []
    for j in range(pairs):
        q = qkv[:, j * 128 : j * 128 + 128] * 0.125
        k = qkv[:, width + j * 128 : width + j * 128 + 128]
        v = qkv[:, 2 * width + j * 128 : 2 * width + j * 128 + 128]
        go = two_heads(g_o2[:, j * 128 : j * 128 + 128])
        p = probs[j]
        g_p = mm_nt(go, v)
        d_v.append(mm_tn(p.astype(BF16), go).astype(BF16))
        d_s = (p * (g_p - jnp.sum(g_p * p, axis=-1, keepdims=True))).astype(BF16)
        d_q.append((mm(side(d_s), two_heads(k)) * 0.125).astype(BF16))
        d_k.append(mm_tn(d_s, two_heads(q)).astype(BF16))
    g_qkv = jnp.concatenate(d_q + d_k + d_v, axis=1)
    for j in range(3):
        grads_ref[at : at + width, :] = mm_tn(a3, g_qkv[:, j * width : (j + 1) * width]).astype(BF16)
        at += width
    d_yn, d_gain_c = rms_back(unit_c, inv_c, gain_c_f, mm_nt(g_qkv, w_qkv[...]))
    g_e = (g_y1 + d_yn).astype(BF16)
    gains_ref[0:1, :] = d_gain_c
    gains_ref[1:2, :] = d_gain_d
    gains_ref[2:8, :] = jnp.zeros((6, width), F32)
    proj_ref[...] = mm_tn(pooled_ref[...], g_e).astype(BF16)
    gpool_ref[...] = mm_nt(g_e, w_proj[...])


def char_backward_kernel(
    sec_ref, chars, lens, gpool, qkv_in, o1_in, x1_in, u1_in, x2_in,
    gain_a, w_qkv, w_out, gain_b, w_up, w_down, gain_p, query_p,
    own_ref, send_ref, grads_ref, gains_ref,
    acc_down, acc_up, acc_out, acc_qkv, acc_gain,
):
    step = pl.program_id(0)
    words, slots, width = chars.shape
    rows = words * slots
    hidden = w_up.shape[1]

    @pl.when(step == 0)
    def _():
        acc_down[...] = jnp.zeros_like(acc_down)
        acc_up[...] = jnp.zeros_like(acc_up)
        acc_out[...] = jnp.zeros_like(acc_out)
        acc_qkv[...] = jnp.zeros_like(acc_qkv)
        acc_gain[...] = jnp.zeros_like(acc_gain)

    lens_now = lens[0]
    gain_pf = gain_p[...].astype(F32)
    query = query_p[...].astype(F32)
    x2 = x2_in[...]
    inv_p, unit_p, normed, weights = pool_forward(x2, gain_pf, query, lens_column(lens_now))
    normed3 = normed.reshape(words, 16, width)
    gp = gpool[...].reshape(words, 1, width)
    g_w = jnp.sum(normed3 * gp, axis=-1, keepdims=True)
    g_r = weights * (g_w - jnp.sum(g_w * weights, axis=1, keepdims=True)) * width ** (-0.5)
    g_n = (weights * gp + g_r * query.reshape(1, 1, width)).reshape(rows, width)
    d_query = jnp.sum((g_r * normed3).reshape(rows, width), axis=0, keepdims=True)
    g_x2, d_gain_p = rms_back(unit_p, inv_p, gain_pf, g_n)
    g_b2 = g_x2.astype(BF16)
    h1, slope = gelu_both(u1_in[...].astype(F32))
    acc_down[...] += mm_tn(g_b2, h1.astype(BF16))
    g_u1 = (slope * mm_nt(g_b2, w_down[...])).astype(BF16)
    gain_bf = gain_b[...].astype(F32)
    x1 = x1_in[...]
    inv_b = inverse_rms(x1)
    unit_b = x1 * inv_b
    acc_up[...] += mm_tn((unit_b * gain_bf).astype(BF16), g_u1)
    d_x1n, d_gain_b = rms_back(unit_b, inv_b, gain_bf, mm_nt(g_u1, w_up[...]))
    g_x1 = g_x2 + d_x1n
    g_c1 = g_x1.astype(BF16)
    acc_out[...] += mm_tn(o1_in[...], g_c1)
    g_o1 = mm_nt(g_c1, w_out[...]).astype(BF16)
    row = lax.broadcasted_iota(jnp.int32, (GROUP, GROUP), 0)
    lane = lax.broadcasted_iota(jnp.int32, (GROUP, GROUP), 1)
    same = (row // 16) == (lane // 16)
    parts = []
    for g in range(rows // GROUP):
        at = slice(g * GROUP, (g + 1) * GROUP)
        allowed = same & ((row % 16) < lens_now[g : g + 1])
        mask = jnp.where(allowed, 0.0, NEGATIVE)
        d_q, d_k, d_v = [], [], []
        for j in range(2):
            q = qkv_in[at, j * 128 : j * 128 + 128] * 0.125
            k = qkv_in[at, width + j * 128 : width + j * 128 + 128]
            v = qkv_in[at, 2 * width + j * 128 : 2 * width + j * 128 + 128]
            go = g_o1[at, j * 128 : j * 128 + 128]
            ks = two_heads(k)
            s = mm_nt(ks, q).reshape(2, GROUP, GROUP) + mask
            e = jnp.exp(s - jnp.max(s, axis=1, keepdims=True))
            p = e * (1.0 / jnp.sum(e, axis=1, keepdims=True))
            g_p = mm_nt(two_heads(v), go).reshape(2, GROUP, GROUP)
            d_s = p * (g_p - jnp.sum(g_p * p, axis=1, keepdims=True))
            d_s = d_s.astype(BF16).reshape(2 * GROUP, GROUP)
            p_low = p.astype(BF16).reshape(2 * GROUP, GROUP)
            d_v.append(mm(side(p_low), two_heads(go)).astype(BF16))
            d_k.append(mm(side(d_s), two_heads(q)).astype(BF16))
            d_q.append((mm_tn(d_s, ks) * 0.125).astype(BF16))
        parts.append(jnp.concatenate(d_q + d_k + d_v, axis=1))
    g_qkv = jnp.concatenate(parts, axis=0)
    gain_af = gain_a[...].astype(F32)
    x = chars[...].reshape(rows, width).astype(F32)
    inv_a = inverse_rms(x)
    unit_a = x * inv_a
    acc_qkv[...] += mm_tn((unit_a * gain_af).astype(BF16), g_qkv)
    d_xn, d_gain_a = rms_back(unit_a, inv_a, gain_af, mm_nt(g_qkv, w_qkv[...]))
    d_chars = (g_x1 + d_xn).astype(BF16).reshape(words, slots, width)
    first = sec_ref[0] == 0
    left, right = d_chars[:, :, : width // 2], d_chars[:, :, width // 2 :]

    @pl.when(first)
    def _():
        own_ref[...] = left
        send_ref[...] = right

    @pl.when(jnp.logical_not(first))
    def _():
        own_ref[...] = right
        send_ref[...] = left

    acc_gain[0:1, :] += d_gain_a
    acc_gain[1:2, :] += d_gain_b
    acc_gain[2:3, :] += d_gain_p
    acc_gain[3:4, :] += d_query

    @pl.when(step == pl.num_programs(0) - 1)
    def _():
        w = width
        down = acc_down[...].astype(BF16).T
        grads_ref[0 : 2 * w, 0:w] = down[0 : 2 * w]
        grads_ref[0 : 2 * w, w : 2 * w] = down[2 * w : 4 * w]
        up = acc_up[...].astype(BF16)
        grads_ref[2 * w : 3 * w, :] = up[:, : 2 * w]
        grads_ref[3 * w : 4 * w, :] = up[:, 2 * w :]
        qkv_g = acc_qkv[...].astype(BF16)
        grads_ref[4 * w : 5 * w, :] = qkv_g[:, : 2 * w]
        grads_ref[5 * w : 6 * w, 0:w] = qkv_g[:, 2 * w :]
        grads_ref[5 * w : 6 * w, w : 2 * w] = acc_out[...].astype(BF16)
        gains_ref[...] = acc_gain[...]


def whole(array):
    return pl.BlockSpec(array.shape, lambda *_: (0,) * array.ndim)


def char_forward(section, chars, lens, weights):
    slots, width = chars.shape[1:]
    words = chars.shape[0] // 2
    rows = words * slots
    steps = words // BLOCK_WORDS
    block = BLOCK_WORDS * slots
    w_proj = weights[-1]
    hidden = weights[4].shape[1]

    def out(n):
        return pl.BlockSpec((block, n), lambda i, s: (i, 0))

    return pl.pallas_call(
        char_forward_kernel,
        grid_spec=pltpu.PrefetchScalarGridSpec(
            num_scalar_prefetch=1,
            grid=(steps,),
            in_specs=[
                pl.BlockSpec((BLOCK_WORDS, slots, width), lambda i, s: (s[0] * steps + i, 0, 0)),
                pl.BlockSpec((1,) + lens.shape[1:], lambda i, s: (s[0] * steps + i, 0, 0)),
            ]
            + [whole(w) for w in weights],
            out_specs=[
                out(3 * width), out(width), out(width), out(hidden), out(width),
                pl.BlockSpec((BLOCK_WORDS, width), lambda i, s: (i, 0)),
                pl.BlockSpec((BLOCK_WORDS, w_proj.shape[1]), lambda i, s: (i, 0)),
            ],
        ),
        out_shape=[
            jax.ShapeDtypeStruct((rows, 3 * width), BF16),
            jax.ShapeDtypeStruct((rows, width), BF16),
            jax.ShapeDtypeStruct((rows, width), F32),
            jax.ShapeDtypeStruct((rows, hidden), BF16),
            jax.ShapeDtypeStruct((rows, width), F32),
            jax.ShapeDtypeStruct((words, width), BF16),
            jax.ShapeDtypeStruct((words, w_proj.shape[1]), BF16),
        ],
        compiler_params=pltpu.CompilerParams(vmem_limit_bytes=50 << 20),
        name="char_forward",
    )(section, chars, lens, *weights)


def word_pass(vector, mask, grad, pooled, weights, w_proj):
    rows, width = vector.shape
    total = sum(w.size for w in weights if w.shape[0] > 1) // width
    operands = (vector, mask, grad, pooled) + weights + (w_proj,)
    return pl.pallas_call(
        word_kernel,
        out_shape=[
            jax.ShapeDtypeStruct((rows, width), BF16),
            jax.ShapeDtypeStruct((total, width), BF16),
            jax.ShapeDtypeStruct((8, width), F32),
            jax.ShapeDtypeStruct(w_proj.shape, BF16),
            jax.ShapeDtypeStruct((rows, w_proj.shape[0]), F32),
        ],
        compiler_params=pltpu.CompilerParams(vmem_limit_bytes=56 << 20),
        name="word_pass",
    )(*operands)


def char_backward(section, chars, lens, gpool, saved, weights):
    slots, width = chars.shape[1:]
    words = chars.shape[0] // 2
    steps = words // BLOCK_WORDS
    block = BLOCK_WORDS * slots
    hidden = weights[4].shape[1]

    def rowed(n):
        return pl.BlockSpec((block, n), lambda i, s: (i, 0))

    half = pl.BlockSpec((BLOCK_WORDS, slots, width // 2), lambda i, s: (i, 0, 0))
    total = (hidden * 2 + 4 * width) // 2
    return pl.pallas_call(
        char_backward_kernel,
        grid_spec=pltpu.PrefetchScalarGridSpec(
            num_scalar_prefetch=1,
            grid=(steps,),
            in_specs=[
                pl.BlockSpec((BLOCK_WORDS, slots, width), lambda i, s: (s[0] * steps + i, 0, 0)),
                pl.BlockSpec((1,) + lens.shape[1:], lambda i, s: (s[0] * steps + i, 0, 0)),
                pl.BlockSpec((BLOCK_WORDS, width), lambda i, s: (i, 0)),
                rowed(3 * width), rowed(width), rowed(width), rowed(hidden), rowed(width),
            ]
            + [whole(w) for w in weights],
            out_specs=[
                half, half,
                pl.BlockSpec((total, 2 * width), lambda i, s: (0, 0)),
                pl.BlockSpec((8, width), lambda i, s: (0, 0)),
            ],
            scratch_shapes=[
                pltpu.VMEM((width, hidden), F32),
                pltpu.VMEM((width, hidden), F32),
                pltpu.VMEM((width, width), F32),
                pltpu.VMEM((width, 3 * width), F32),
                pltpu.VMEM((8, width), F32),
            ],
        ),
        out_shape=[
            jax.ShapeDtypeStruct((words, slots, width // 2), BF16),
            jax.ShapeDtypeStruct((words, slots, width // 2), BF16),
            jax.ShapeDtypeStruct((total, 2 * width), BF16),
            jax.ShapeDtypeStruct((8, width), F32),
        ],
        compiler_params=pltpu.CompilerParams(vmem_limit_bytes=50 << 20),
        name="char_backward",
    )(section, chars, lens, gpool, *saved, *weights)


AXES = ("section", "dp")


def exchange(value, partner):
    dp = lax.axis_size("dp")
    pairs = []
    for s in range(lax.axis_size("section")):
        for d in range(dp):
            t, e = partner(s, d)
            pairs.append((s * dp + d, t * dp + e))
    return lax.ppermute(value, AXES, pairs)


def by_core(first, second):
    return lambda s, d: first(s, d) if d % 2 == 0 else second(s, d)


def flip_section(s, d):
    return 1 - s, d


def flip_bit(bit):
    return lambda s, d: (s, d ^ (1 << bit))


def sum_all(value):
    sec = lax.axis_index("section")
    dp = lax.axis_index("dp")
    core = dp & 1
    x = (dp >> 1) & 1
    bits = lax.axis_size("dp").bit_length() - 1
    stages = [
        (flip_bit(0), core),
        (by_core(flip_bit(1), flip_section), jnp.where(core == 0, x, sec)),
        (by_core(flip_section, flip_bit(1)), jnp.where(core == 0, sec, x)),
        (flip_bit(2), (dp >> 2) & 1),
        (flip_bit(3), (dp >> 3) & 1),
    ]
    for partner, bit in stages:
        n = value.shape[0] // 2
        keep = lax.dynamic_slice_in_dim(value, bit * n, n, 0)
        send = lax.dynamic_slice_in_dim(value, (1 - bit) * n, n, 0)
        value = (keep.astype(F32) + exchange(send, partner).astype(F32)).astype(BF16)
    for extra in range(4, bits):
        value = (value.astype(F32) + exchange(value, flip_bit(extra)).astype(F32)).astype(BF16)
    for partner, bit in reversed(stages):
        other = exchange(value, partner)
        value = jnp.concatenate(
            [jnp.where(bit == 0, value, other), jnp.where(bit == 0, other, value)], axis=0
        )
    return value


def body(
    chars, char_lengths, word_mask, out_grad, char_gain_a, char_qkv, char_out, char_gain_b, char_up,
    char_down, pool_gain, pool_query, char_proj, word_gain_a, word_qkv, word_out, word_gain_b,
    word_up, word_down,
):
    def flat(v):
        return v.reshape(1, -1)

    slots, cwidth = chars.shape[1:]
    words = chars.shape[0] // 2
    width = word_qkv.shape[0]
    sec = lax.axis_index("section")
    section = sec.astype(jnp.int32).reshape(1)
    lens = jnp.repeat(char_lengths, slots).reshape(-1, BLOCK_WORDS * slots // GROUP, GROUP)
    char_weights = (
        flat(char_gain_a), char_qkv, char_out, flat(char_gain_b), char_up, char_down,
        flat(pool_gain), flat(pool_query), char_proj,
    )
    word_weights = (flat(word_gain_a), word_qkv, word_out, flat(word_gain_b), word_up, word_down)
    *saved, pooled, vector = char_forward(section, chars, lens, char_weights)
    mask = lax.dynamic_slice_in_dim(word_mask, sec * words, words).reshape(1, words)
    grad = lax.dynamic_slice_in_dim(out_grad, sec * words, words, 0)
    result, word_grads, word_gains, proj_grad, gpool = word_pass(
        vector, mask, grad, pooled, word_weights, char_proj
    )
    word_sum = sum_all(word_grads).astype(F32)
    half = width // 2
    own_out = jnp.where(sec == 0, result[:, :half], result[:, half:])
    send_out = jnp.where(sec == 0, result[:, half:], result[:, :half])
    got_out = exchange(send_out, flip_section)
    word_outputs = jnp.concatenate(
        [jnp.where(sec == 0, own_out, got_out), jnp.where(sec == 0, got_out, own_out)], axis=0
    )
    own, send, char_grads, char_gains = char_backward(
        section, chars, lens, gpool, saved, char_weights[:-1]
    )
    got = exchange(send, flip_section)
    char_grad = jnp.concatenate([jnp.where(sec == 0, own, got), jnp.where(sec == 0, got, own)], axis=0)
    gains = jnp.concatenate([word_gains, char_gains.reshape(-1, width)], axis=0)
    rows = proj_grad.shape[0] + char_grads.shape[0] + gains.shape[0]
    pad = jnp.zeros((-rows % 512, width), BF16)
    rest = sum_all(jnp.concatenate([proj_grad, char_grads, gains.astype(BF16), pad], axis=0)).astype(F32)
    hidden = word_up.shape[1]
    d_word_down = word_sum[:hidden]
    at = hidden
    d_word_up = jnp.concatenate([word_sum[at + j * width : at + (j + 1) * width] for j in range(hidden // width)], axis=1)
    at += hidden
    d_word_out = word_sum[at : at + width]
    at += width
    d_word_qkv = jnp.concatenate([word_sum[at + j * width : at + (j + 1) * width] for j in range(3)], axis=1)
    w = cwidth
    d_proj = rest[:w]
    rest = rest[w:]
    d_down = jnp.concatenate([rest[: 2 * w, :w], rest[: 2 * w, w:]], axis=0)
    d_up = jnp.concatenate([rest[2 * w : 3 * w], rest[3 * w : 4 * w]], axis=1)
    d_qkv = jnp.concatenate([rest[4 * w : 5 * w], rest[5 * w : 6 * w, :w]], axis=1)
    d_out = rest[5 * w : 6 * w, w:]
    gains = rest[6 * w :]
    cg = gains[8:12].reshape(-1, w)
    return (
        word_outputs, char_grad, cg[0], d_qkv, d_out, cg[1], d_up, d_down, cg[2], cg[3], d_proj,
        gains[0], d_word_qkv, d_word_out, gains[1], d_word_up, d_word_down,
    )


def solution(mesh):
    return jax.shard_map(
        body,
        mesh=mesh,
        in_specs=(P("dp", None, None), P("dp"), P("dp"), P("dp", None)) + (P(),) * 15,
        out_specs=(P("dp", "section"), P("dp", None, "section")) + (P(),) * 15,
        check_vma=False,
    )
```

time: 1140 us -> 297 us (0.26); the launches traced: 1120 us -> 296 us
  matrix products: 305 us -> 0 us
  local copies, waits for them, and re-layouts: 326 us -> 38.1 us
  other arithmetic: 166 us -> 43.1 us
  blocking collectives: 116 us -> 0 us
  Pallas kernels: 0 us -> 102 us
  waiting for transfers between devices: 167 us -> 82.6 us
  between operations: 14.6 us -> 1.17 us
    dot_general x52 -> x0, matrix products: 305 us -> none  [the longest x16 98.2 us: product(): return jnp.dot(left, right, preferred_element_type=jnp.float32)]
    psum x1 -> x0, waiting for transfers between devices: 159 us -> none  [body(): summed = lax.psum(char_grads + word_grads, ('section', 'dp'))]
    psum x1 -> x0, blocking collectives: 116 us -> none  [body(): summed = lax.psum(char_grads + word_grads, ('section', 'dp'))]
    pallas_call x0 -> x3, Pallas kernels: none -> 102 us  [the longest x1 58.6 us: char_backward(): pl.pallas_call(char_backward_kernel, grid_spec=pltpu.PrefetchScalarGridSp...]
    cond x124 -> x0, local copies, waits for them, and re-layouts: 102 us -> none
    another operation x22 -> x0, local copies, waits for them, and re-layouts: 77.5 us -> none
    ppermute x5 -> x22, waiting for transfers between devices: 7.88 us -> 82.6 us  [exchange(): return lax.ppermute(value, AXES, pairs)]
    convert_element_type x10 -> x0, local copies, waits for them, and re-layouts: 68.4 us -> none  [rounded(): return value.astype(jnp.bfloat16)]
  transfers between devices with their start and end apart: 6 -> 22, of which waited for: 2 -> 12; matrix products, arithmetic and copies ran while one was open for 34% -> 11% of each run, Pallas kernels for 0% -> 20%
where the time goes in v1:
time: 297 us; the launch traced here: 296 us
  Pallas kernels  102 us (34%)
  waiting for transfers between devices  82.6 us (28%)
  other arithmetic  43.1 us (15%)
  local copies, waits for them, and re-layouts  38.1 us (13%)
  starting transfers between devices  29.2 us (10%)
    ppermute x22, waiting for transfers between devices, exchange(): return lax.ppermute(value, AXES, pairs)  82.6 us
    pallas_call x1, Pallas kernels, char_backward(): pl.pallas_call(char_backward_kernel, grid_spec=pltpu.PrefetchScalarGridSp...  58.6 us
    pallas_call x1, Pallas kernels, char_forward(): pl.pallas_call(char_forward_kernel, grid_spec=pltpu.PrefetchScalarGridSpe...  29.3 us
    ppermute x22, starting transfers between devices, exchange(): return lax.ppermute(value, AXES, pairs)  29.2 us
    pallas_call x1, Pallas kernels, word_pass(): pl.pallas_call(word_kernel, out_shape=[jax.ShapeDtypeStruct((rows, width)...  14.4 us
    unnamed x56, local copies, waits for them, and re-layouts  12.7 us
    convert_element_type x10, other arithmetic, sum_all(): (keep.astype(F32) + exchange(send, partner).astype(F32)).astype(BF16)  11.6 us
    select_n x10, other arithmetic, sum_all(): jnp.where(bit == 0, value, other)  8.19 us
  transfers between devices with their start and end apart: 22, of which 12 were waited for; matrix products, arithmetic and copies ran while one was open for 11% of the time, Pallas kernels for 20%

profile of v1, /device:TPU:1, one launch (start us, length us, event | category | flops | bytes accessed | tf_op | source)
XLA Modules:
  0.0 296.4 jit_solution(4715702920272017455)
XLA Ops:
  4.4 1.3 dynamic_slice.66
  6.5 1.3 reshape.73.gain_c
  7.7 1.3 reshape.74.gain_d
  13.9 29.3 %char_forward.1 = (bf16[4096,768]{1,0:T(8,128)(2,1)}, bf16[4096,256]{1,0:T(8,128)(2,1)}, f32[4096,256]{1,0:T(8,128)}, bf16[4096,1024]{1,0:T(8,128)(2,1)}, f32[40...) custom-call(s32[1]{0:T(128)} %bitcast.sec_ref, bf16[512,16,256]{2,1,0:T(8,128)(2,1)} %chars.3, ...), custom_call_target="tpu_custom_call" | custom-call | tf_op jit(solution)/shard_map/char_forward/pallas_call | solution.py:343
  44.6 14.4 %word_pass.1 = (bf16[256,512]{1,0:T(8,128)(2,1)}, bf16[6144,512]{1,0:T(8,128)(2,1)}, f32[8,512]{1,0:T(8,128)}, bf16[256,512]{1,0:T(8,128)(2,1)}, f32[256,256]{1,0:T(8,128)}) custom-call(bf16[256,512]{1,0:T(8,128)(2,1)} %copy-done.12, s32[1,256]{1,0:T(1,128)} %bitcast.10, bf16[256,512]{1,0:T(8,128)(2,1)} %constant_dynamic-slice_fusion.10.g_ref, ...), custom_call_target="tpu_custom_call" | custom-call | tf_op jit(solution)/shard_map/word_pass/pallas_call | solution.py:377
  59.0 3.8 %constant_dynamic-slice_fusion.4 = bf16[3072,512]{1,0:T(8,128)(2,1)} fusion(bf16[6144,512]{1,0:T(8,128)(2,1)} %get-tuple-element.48, s32[]{:T(128)S(6)} %select_n.267), kind=kLoop, calls=%fused_computation.68 | loop fusion | bytes 6291460 | tf_op jit(solution)/shard_map/dynamic_slice | solution.py:480
  62.8 6.0 %collective-permute-done.12 = bf16[3072,512]{1,0:T(8,128)(2,1)} collective-permute-done((bf16[3072,512]{1,0:T(8,128)(2,1)}, bf16[3072,512]{1,0:T(8,128)(2,1)}, u32[]{:S(2)}, u32[]{:S(2)}) %collective-permute-start.12) | collective-permute-done | bytes 3145760 | tf_op jit(solution)/shard_map/ppermute | solution.py:449
  68.7 3.7 %add_convert_fusion = bf16[3072,512]{1,0:T(8,128)(2,1)S(1)} fusion(bf16[3072,512]{1,0:T(8,128)(2,1)} %collective-permute-done.12, bf16[6144,512]{1,0:T(8,128)(2,1)} %get-tuple-element.48, s32[]{:T(128)S(6)} %select_n.266), kind=kLoop, calls=%fused_computation | loop fusion | flops 6291456 | bytes 9437188 | tf_op jit(solution)/shard_map/convert_element_type | solution.py:481
  72.5 1.7 copy-done.20
  74.2 1.2 constant_dynamic-slice_fusion.3
  75.4 2.4 collective-permute-start.13
  77.8 58.6 %char_backward.1 = (bf16[256,16,128]{2,1,0:T(8,128)(2,1)S(1)}, bf16[256,16,128]{2,1,0:T(8,128)(2,1)S(1)}, bf16[1536,512]{1,0:T(8,128)(2,1)}, f32[8,256]{1,0:T(8,128)S(1)}) custom-call(s32[1]{0:T(128)} %bitcast.sec_ref, bf16[512,16,256]{2,1,0:T(8,128)(2,1)} %chars.3, s32[16,4,128]{2,1,0:T(4,128)S(1)} %broadcast_in_dim.12.lens, f32[256,256]{1,0:T(8,128)S(1)} %copy-done.11, ...), custom_call_target="tpu_custom_call" | custom-call | tf_op jit(solution)/shard_map/char_backward/pallas_call | solution.py:403
  137.4 7.4 %concatenate.59 = bf16[2048,512]{1,0:T(8,128)(2,1)S(1)} concatenate(bf16[256,512]{1,0:T(8,128)(2,1)} %get-tuple-element.44, bf16[1536,512]{1,0:T(8,128)(2,1)} %get-tuple-element.45, bf16[8,512]{1,0:T(8,128)(2,1)S(1)} %convert.7, bf16[4,512]{1,0:T(4,128)(2,1)S(1)} %reshape.75, bf16[244,512]{1,0:T(8,128)(2,1)S(1)} %broadcast_in_dim.13), dimensions={0} | concatenate | bytes 4194304 | tf_op jit(solution)/shard_map/concatenate | solution.py:533
  144.8 2.3 add_convert_fusion.1
  152.4 8.3 %collective-permute-done.14 = bf16[768,512]{1,0:T(8,128)(2,1)} collective-permute-done((bf16[768,512]{1,0:T(8,128)(2,1)}, bf16[768,512]{1,0:T(8,128)(2,1)}, u32[]{:S(2)}, u32[]{:S(2)}) %collective-permute-start.14) | collective-permute-done | bytes 786464 | tf_op jit(solution)/shard_map/ppermute | solution.py:449
  160.6 1.6 add_convert_fusion.3
  163.1 1.3 collective-permute-start.15
  164.4 1.5 add_convert_fusion.2
  167.6 4.9 %collective-permute-done.15 = bf16[384,512]{1,0:T(8,128)(2,1)S(1)} collective-permute-done((bf16[384,512]{1,0:T(8,128)(2,1)}, bf16[384,512]{1,0:T(8,128)(2,1)S(1)}, u32[]{:S(2)}, u32[]{:S(2)}) %collective-permute-start.15) | collective-permute-done | bytes 393248 | tf_op jit(solution)/shard_map/ppermute | solution.py:449
  173.6 2.4 collective-permute-start.16
  177.2 2.3 collective-permute-start.4
  179.4 5.1 %collective-permute-done.16 = bf16[192,512]{1,0:T(8,128)(2,1)S(1)} collective-permute-done((bf16[192,512]{1,0:T(8,128)(2,1)S(1)}, bf16[192,512]{1,0:T(8,128)(2,1)S(1)}, u32[]{:S(2)}, u32[]{:S(2)}) %collective-permute-start.16) | collective-permute-done | bytes 196640 | tf_op jit(solution)/shard_map/ppermute | solution.py:449
  184.8 3.8 %collective-permute-start.5 = (bf16[128,512]{1,0:T(8,128)(2,1)S(1)}, bf16[128,512]{1,0:T(8,128)(2,1)S(1)}, u32[]{:S(2)}, u32[]{:S(2)}) collective-permute-start(bf16[128,512]{1,0:T(8,128)(2,1)S(1)} %constant_dynamic-slice_fusion.6), channel_id=1, source_target_pairs={{0,4},{1,5},{2,6},{3,7},{4,0},{5,1},{6,2},{7,3},{8,12},{9,13},{10,... | collective-permute-start | bytes 393224 | tf_op jit(solution)/shard_map/ppermute | solution.py:449
  188.6 6.8 %collective-permute-done.17 = bf16[192,512]{1,0:T(8,128)(2,1)S(1)} collective-permute-done((bf16[192,512]{1,0:T(8,128)(2,1)S(1)}, bf16[192,512]{1,0:T(8,128)(2,1)S(1)}, u32[]{:S(2)}, u32[]{:S(2)}) %collective-permute-start.17) | collective-permute-done | bytes 196640 | tf_op jit(solution)/shard_map/ppermute | solution.py:449
  195.6 2.4 collective-permute-start.6
  198.0 8.6 %collective-permute-done.18 = bf16[384,512]{1,0:T(8,128)(2,1)S(1)} collective-permute-done((bf16[384,512]{1,0:T(8,128)(2,1)S(1)}, bf16[384,512]{1,0:T(8,128)(2,1)S(1)}, u32[]{:S(2)}, u32[]{:S(2)}) %collective-permute-start.18) | collective-permute-done | bytes 393248 | tf_op jit(solution)/shard_map/ppermute | solution.py:449
  206.9 3.0 %collective-permute-start.7 = (bf16[64,512]{1,0:T(8,128)(2,1)S(1)}, bf16[64,512]{1,0:T(8,128)(2,1)S(1)}, u32[]{:S(2)}, u32[]{:S(2)}) collective-permute-start(bf16[64,512]{1,0:T(8,128)(2,1)S(1)} %add_convert_fusion.9), channel_id=1, source_target_pairs={{0,8},{1,9},{2,10},{3,11},{4,12},{5,13},{6,14},{7,15},{8,0},{9,1},... | collective-permute-start | bytes 196616 | tf_op jit(solution)/shard_map/ppermute | solution.py:449
  209.9 1.9 collective-permute-done.7
  211.8 2.9 collective-permute-start.8
  214.7 2.8 collective-permute-done.8
  218.1 1.4 broadcast_select_fusion.9
  220.4 1.2 pad_maximum_fusion.5
  221.8 1.2 collective-permute-start.9
  223.1 4.0 %collective-permute-done.9 = bf16[256,512]{1,0:T(8,128)(2,1)S(1)} collective-permute-done((bf16[256,512]{1,0:T(8,128)(2,1)S(1)}, bf16[256,512]{1,0:T(8,128)(2,1)S(1)}, u32[]{:S(2)}, u32[]{:S(2)}) %collective-permute-start.9) | collective-permute-done | bytes 262176 | tf_op jit(solution)/shard_map/ppermute | solution.py:449
  228.0 2.4 collective-permute-start.10
  231.5 1.4 collective-permute-start.1
  233.0 25.9 %collective-permute-done.10 = bf16[512,512]{1,0:T(8,128)(2,1)} collective-permute-done((bf16[512,512]{1,0:T(8,128)(2,1)}, bf16[512,512]{1,0:T(8,128)(2,1)}, u32[]{:S(2)}, u32[]{:S(2)}) %collective-permute-start.10) | collective-permute-done | bytes 524320 | tf_op jit(solution)/shard_map/ppermute | solution.py:449
  258.8 1.2 broadcast_select_fusion.11
  260.2 2.0 broadcast_select_fusion.3
  262.3 1.9 pad_maximum_fusion.1
  267.1 7.8 %collective-permute-done.1 = bf16[256,16,128]{2,1,0:T(8,128)(2,1)} collective-permute-done((bf16[256,16,128]{2,1,0:T(8,128)(2,1)S(1)}, bf16[256,16,128]{2,1,0:T(8,128)(2,1)}, u32[]{:S(2)}, u32[]{:S(2)}) %collective-permute-start.1) | collective-permute-done | bytes 1048608 | tf_op jit(solution)/shard_map/ppermute | solution.py:449
  274.9 1.4 broadcast_select_fusion.7
  276.3 1.5 pad_maximum_fusion.4
  284.9 2.7 broadcast_select_fusion.1
  287.6 1.9 maximum_convert_fusion.4
  289.5 2.6 fusion
  292.1 1.9 pad_maximum_fusion.2
  294.0 2.4 pad_maximum_fusion
  (129 shorter events, 36.5 us)
Async XLA Ops:
  0.7 5.1 %copy-start = (bf16[512,512]{1,0:T(8,128)(2,1)S(1)}, bf16[512,512]{1,0:T(8,128)(2,1)}, u32[]{:S(2)}) copy-start(bf16[512,512]{1,0:T(8,128)(2,1)} %param.22) | copy-start | bytes 1572868
  9.0 1.0 copy-start.2
  10.0 1.0 copy-start.4
  11.1 1.0 copy-start.6
  12.1 0.9 copy-start.8
  13.0 0.9 copy-start.9
  62.7 6.0 %collective-permute-start.12 = (bf16[3072,512]{1,0:T(8,128)(2,1)}, bf16[3072,512]{1,0:T(8,128)(2,1)}, u32[]{:S(2)}, u32[]{:S(2)}) collective-permute-start(bf16[3072,512]{1,0:T(8,128)(2,1)} %constant_dynamic-slice_fusion.4), channel_id=1, source_target_pairs={{0,1},{1,0},{2,3},{3,2},{4,5},{5,4},{6,7},{7,6},{8,9},{9,8},{10,11... | collective-permute-start | bytes 9437192 | tf_op jit(solution)/shard_map/ppermute | solution.py:449
  72.5 1.7 copy-start.20
  74.1 3.6 %copy-start.27 = (f32[8,512]{1,0:T(8,128)S(1)}, f32[8,512]{1,0:T(8,128)}, u32[]{:S(2)}) copy-start(f32[8,512]{1,0:T(8,128)} %get-tuple-element.46) | copy-start | bytes 49156
  74.1 3.6 %copy-start.3 = (bf16[256,1024]{1,0:T(8,128)(2,1)S(1)}, bf16[256,1024]{1,0:T(8,128)(2,1)}, u32[]{:S(2)}) copy-start(bf16[256,1024]{1,0:T(8,128)(2,1)} %w_up.5) | copy-start | bytes 1572868
  74.1 3.6 %copy-start.5 = (bf16[1024,256]{1,0:T(8,128)(2,1)S(1)}, bf16[1024,256]{1,0:T(8,128)(2,1)}, u32[]{:S(2)}) copy-start(bf16[1024,256]{1,0:T(8,128)(2,1)} %w_down.5) | copy-start | bytes 1572868
  74.1 3.7 %copy-start.7 = (bf16[256,768]{1,0:T(8,128)(2,1)S(1)}, bf16[256,768]{1,0:T(8,128)(2,1)}, u32[]{:S(2)}) copy-start(bf16[256,768]{1,0:T(8,128)(2,1)} %w_qkv.5) | copy-start | bytes 1179652
  74.1 3.7 %copy-start.10 = (bf16[256,256]{1,0:T(8,128)(2,1)S(1)}, bf16[256,256]{1,0:T(8,128)(2,1)}, u32[]{:S(2)}) copy-start(bf16[256,256]{1,0:T(8,128)(2,1)} %w_out.5) | copy-start | bytes 393220
  74.2 3.7 %copy-start.11 = (f32[256,256]{1,0:T(8,128)S(1)}, f32[256,256]{1,0:T(8,128)}, u32[]{:S(2)}) copy-start(f32[256,256]{1,0:T(8,128)} %get-tuple-element.36.gpool) | copy-start | bytes 786436
  75.4 69.4 %collective-permute-start.13 = (bf16[1536,512]{1,0:T(8,128)(2,1)}, bf16[1536,512]{1,0:T(8,128)(2,1)}, u32[]{:S(2)}, u32[]{:S(2)}) collective-permute-start(bf16[1536,512]{1,0:T(8,128)(2,1)} %constant_dynamic-slice_fusion.3), channel_id=1, source_target_pairs={{0,2},{1,17},{2,0},{3,19},{4,6},{5,21},{6,4},{7,23},{8,10},{9,25},... | collective-permute-start | bytes 4718600 | tf_op jit(solution)/shard_map/ppermute | solution.py:449
  136.4 1.0 copy-start.14
  147.1 1.1 copy-start.23
  149.2 11.5 %collective-permute-start.14 = (bf16[768,512]{1,0:T(8,128)(2,1)}, bf16[768,512]{1,0:T(8,128)(2,1)}, u32[]{:S(2)}, u32[]{:S(2)}) collective-permute-start(bf16[768,512]{1,0:T(8,128)(2,1)} %constant_dynamic-slice_fusion.2), channel_id=1, source_target_pairs={{0,16},{1,3},{2,18},{3,1},{4,20},{5,7},{6,22},{7,5},{8,24},{9,11},... | collective-permute-start | bytes 2359304 | tf_op jit(solution)/shard_map/ppermute | solution.py:449
  151.4 13.0 %collective-permute-start.2 = (bf16[1024,512]{1,0:T(8,128)(2,1)}, bf16[1024,512]{1,0:T(8,128)(2,1)}, u32[]{:S(2)}, u32[]{:S(2)}) collective-permute-start(bf16[1024,512]{1,0:T(8,128)(2,1)} %constant_dynamic-slice_fusion.9), channel_id=1, source_target_pairs={{0,1},{1,0},{2,3},{3,2},{4,5},{5,4},{6,7},{7,6},{8,9},{9,8},{10,11... | collective-permute-start | bytes 3145736 | tf_op jit(solution)/shard_map/ppermute | solution.py:449
  162.2 2.2 copy-start.25
  163.1 9.3 %collective-permute-start.15 = (bf16[384,512]{1,0:T(8,128)(2,1)}, bf16[384,512]{1,0:T(8,128)(2,1)S(1)}, u32[]{:S(2)}, u32[]{:S(2)}) collective-permute-start(bf16[384,512]{1,0:T(8,128)(2,1)} %constant_dynamic-slice_fusion.1), channel_id=1, source_target_pairs={{0,4},{1,5},{2,6},{3,7},{4,0},{5,1},{6,2},{7,3},{8,12},{9,13},{10,... | collective-permute-start | bytes 1179656 | tf_op jit(solution)/shard_map/ppermute | solution.py:449
  165.9 1.0 copy-start.24
  167.0 9.0 %collective-permute-start.3 = (bf16[512,512]{1,0:T(8,128)(2,1)S(1)}, bf16[512,512]{1,0:T(8,128)(2,1)S(1)}, u32[]{:S(2)}, u32[]{:S(2)}) collective-permute-start(bf16[512,512]{1,0:T(8,128)(2,1)S(1)} %constant_dynamic-slice_fusion.8), channel_id=1, source_target_pairs={{0,2},{1,17},{2,0},{3,19},{4,6},{5,21},{6,4},{7,23},{8,10},{9,25},... | collective-permute-start | bytes 1572872 | tf_op jit(solution)/shard_map/ppermute | solution.py:449
  173.6 10.9 %collective-permute-start.16 = (bf16[192,512]{1,0:T(8,128)(2,1)S(1)}, bf16[192,512]{1,0:T(8,128)(2,1)S(1)}, u32[]{:S(2)}, u32[]{:S(2)}) collective-permute-start(bf16[192,512]{1,0:T(8,128)(2,1)S(1)} %constant_dynamic-slice_fusion), channel_id=1, source_target_pairs={{0,8},{1,9},{2,10},{3,11},{4,12},{5,13},{6,14},{7,15},{8,0},{9,1},... | collective-permute-start | bytes 589832 | tf_op jit(solution)/shard_map/ppermute | solution.py:449
  177.2 7.5 %collective-permute-start.4 = (bf16[256,512]{1,0:T(8,128)(2,1)S(1)}, bf16[256,512]{1,0:T(8,128)(2,1)S(1)}, u32[]{:S(2)}, u32[]{:S(2)}) collective-permute-start(bf16[256,512]{1,0:T(8,128)(2,1)S(1)} %constant_dynamic-slice_fusion.7), channel_id=1, source_target_pairs={{0,16},{1,3},{2,18},{3,1},{4,20},{5,7},{6,22},{7,5},{8,24},{9,11},... | collective-permute-start | bytes 786440 | tf_op jit(solution)/shard_map/ppermute | solution.py:449
  184.6 10.8 %collective-permute-start.17 = (bf16[192,512]{1,0:T(8,128)(2,1)S(1)}, bf16[192,512]{1,0:T(8,128)(2,1)S(1)}, u32[]{:S(2)}, u32[]{:S(2)}) collective-permute-start(bf16[192,512]{1,0:T(8,128)(2,1)S(1)} %add_convert_fusion.7), channel_id=1, source_target_pairs={{0,8},{1,9},{2,10},{3,11},{4,12},{5,13},{6,14},{7,15},{8,0},{9,1},... | collective-permute-start | bytes 589832 | tf_op jit(solution)/shard_map/ppermute | solution.py:449
  184.8 10.8 %collective-permute-start.5 = (bf16[128,512]{1,0:T(8,128)(2,1)S(1)}, bf16[128,512]{1,0:T(8,128)(2,1)S(1)}, u32[]{:S(2)}, u32[]{:S(2)}) collective-permute-start(bf16[128,512]{1,0:T(8,128)(2,1)S(1)} %constant_dynamic-slice_fusion.6), channel_id=1, source_target_pairs={{0,4},{1,5},{2,6},{3,7},{4,0},{5,1},{6,2},{7,3},{8,12},{9,13},{10,... | collective-permute-start | bytes 393224 | tf_op jit(solution)/shard_map/ppermute | solution.py:449
  195.5 11.1 %collective-permute-start.18 = (bf16[384,512]{1,0:T(8,128)(2,1)S(1)}, bf16[384,512]{1,0:T(8,128)(2,1)S(1)}, u32[]{:S(2)}, u32[]{:S(2)}) collective-permute-start(bf16[384,512]{1,0:T(8,128)(2,1)S(1)} %pad_maximum_fusion.12), channel_id=1, source_target_pairs={{0,4},{1,5},{2,6},{3,7},{4,0},{5,1},{6,2},{7,3},{8,12},{9,13},{10,... | collective-permute-start | bytes 1179656 | tf_op jit(solution)/shard_map/ppermute | solution.py:449
  195.6 11.2 %collective-permute-start.6 = (bf16[64,512]{1,0:T(8,128)(2,1)S(1)}, bf16[64,512]{1,0:T(8,128)(2,1)S(1)}, u32[]{:S(2)}, u32[]{:S(2)}) collective-permute-start(bf16[64,512]{1,0:T(8,128)(2,1)S(1)} %constant_dynamic-slice_fusion.5), channel_id=1, source_target_pairs={{0,8},{1,9},{2,10},{3,11},{4,12},{5,13},{6,14},{7,15},{8,0},{9,1},... | collective-permute-start | bytes 196616 | tf_op jit(solution)/shard_map/ppermute | solution.py:449
  206.8 11.3 %collective-permute-start.19 = (bf16[768,512]{1,0:T(8,128)(2,1)S(1)}, bf16[768,512]{1,0:T(8,128)(2,1)}, u32[]{:S(2)}, u32[]{:S(2)}) collective-permute-start(bf16[768,512]{1,0:T(8,128)(2,1)S(1)} %pad_maximum_fusion.10), channel_id=1, source_target_pairs={{0,16},{1,3},{2,18},{3,1},{4,20},{5,7},{6,22},{7,5},{8,24},{9,11},... | collective-permute-start | bytes 2359304 | tf_op jit(solution)/shard_map/ppermute | solution.py:449
  206.9 4.9 %collective-permute-start.7 = (bf16[64,512]{1,0:T(8,128)(2,1)S(1)}, bf16[64,512]{1,0:T(8,128)(2,1)S(1)}, u32[]{:S(2)}, u32[]{:S(2)}) collective-permute-start(bf16[64,512]{1,0:T(8,128)(2,1)S(1)} %add_convert_fusion.9), channel_id=1, source_target_pairs={{0,8},{1,9},{2,10},{3,11},{4,12},{5,13},{6,14},{7,15},{8,0},{9,1},... | collective-permute-start | bytes 196616 | tf_op jit(solution)/shard_map/ppermute | solution.py:449
  211.8 5.6 %collective-permute-start.8 = (bf16[128,512]{1,0:T(8,128)(2,1)S(1)}, bf16[128,512]{1,0:T(8,128)(2,1)S(1)}, u32[]{:S(2)}, u32[]{:S(2)}) collective-permute-start(bf16[128,512]{1,0:T(8,128)(2,1)S(1)} %pad_maximum_fusion.15), channel_id=1, source_target_pairs={{0,4},{1,5},{2,6},{3,7},{4,0},{5,1},{6,2},{7,3},{8,12},{9,13},{10,... | collective-permute-start | bytes 393224 | tf_op jit(solution)/shard_map/ppermute | solution.py:449
  219.5 0.9 copy-start.21
  219.5 12.0 %copy-start.15 = (bf16[256,16,128]{2,1,0:T(8,128)(2,1)S(1)}, bf16[256,16,128]{2,1,0:T(8,128)(2,1)}, u32[]{:S(2)}) copy-start(bf16[256,16,128]{2,1,0:T(8,128)(2,1)} %copy-done.14) | copy-start | bytes 3145732
  221.6 38.6 %collective-permute-start.20 = (bf16[1536,512]{1,0:T(8,128)(2,1)}, bf16[1536,512]{1,0:T(8,128)(2,1)}, u32[]{:S(2)}, u32[]{:S(2)}) collective-permute-start(bf16[1536,512]{1,0:T(8,128)(2,1)} %pad_maximum_fusion.5), channel_id=1, source_target_pairs={{0,2},{1,17},{2,0},{3,19},{4,6},{5,21},{6,4},{7,23},{8,10},{9,25},... | collective-permute-start | bytes 4718600 | tf_op jit(solution)/shard_map/ppermute | solution.py:449
  221.8 5.3 %collective-permute-start.9 = (bf16[256,512]{1,0:T(8,128)(2,1)S(1)}, bf16[256,512]{1,0:T(8,128)(2,1)S(1)}, u32[]{:S(2)}, u32[]{:S(2)}) collective-permute-start(bf16[256,512]{1,0:T(8,128)(2,1)S(1)} %pad_maximum_fusion.14), channel_id=1, source_target_pairs={{0,16},{1,3},{2,18},{3,1},{4,20},{5,7},{6,22},{7,5},{8,24},{9,11},... | collective-permute-start | bytes 786440 | tf_op jit(solution)/shard_map/ppermute | solution.py:449
  228.0 30.8 %collective-permute-start.10 = (bf16[512,512]{1,0:T(8,128)(2,1)}, bf16[512,512]{1,0:T(8,128)(2,1)}, u32[]{:S(2)}, u32[]{:S(2)}) collective-permute-start(bf16[512,512]{1,0:T(8,128)(2,1)} %pad_maximum_fusion.11), channel_id=1, source_target_pairs={{0,2},{1,17},{2,0},{3,19},{4,6},{5,21},{6,4},{7,23},{8,10},{9,25},... | collective-permute-start | bytes 1572872 | tf_op jit(solution)/shard_map/ppermute | solution.py:449
  231.4 34.0 %collective-permute-start = (bf16[256,256]{1,0:T(8,128)(2,1)S(1)}, bf16[256,256]{1,0:T(8,128)(2,1)}, u32[]{:S(2)}, u32[]{:S(2)}) collective-permute-start(bf16[256,256]{1,0:T(8,128)(2,1)S(1)} %broadcast_select_fusion.22), channel_id=1, source_target_pairs={{0,16},{1,17},{2,18},{3,19},{4,20},{5,21},{6,22},{7,23},{8,24},{9,... | collective-permute-start | bytes 393224 | tf_op jit(solution)/shard_map/ppermute | solution.py:449
  231.5 43.4 %collective-permute-start.1 = (bf16[256,16,128]{2,1,0:T(8,128)(2,1)S(1)}, bf16[256,16,128]{2,1,0:T(8,128)(2,1)}, u32[]{:S(2)}, u32[]{:S(2)}) collective-permute-start(bf16[256,16,128]{2,1,0:T(8,128)(2,1)S(1)} %copy-done.15), channel_id=1, source_target_pairs={{0,16},{1,17},{2,18},{3,19},{4,20},{5,21},{6,22},{7,23},{8,24},{9,... | collective-permute-start | bytes 3145736 | tf_op jit(solution)/shard_map/ppermute | solution.py:449
  233.0 27.3 %copy-start.22 = (bf16[768,512]{1,0:T(8,128)(2,1)S(1)}, bf16[768,512]{1,0:T(8,128)(2,1)}, u32[]{:S(2)}) copy-start(bf16[768,512]{1,0:T(8,128)(2,1)} %copy-done.21) | copy-start | bytes 2359300
  260.1 17.7 %collective-permute-start.11 = (bf16[1024,512]{1,0:T(8,128)(2,1)S(1)}, bf16[1024,512]{1,0:T(8,128)(2,1)S(1)}, u32[]{:S(2)}, u32[]{:S(2)}) collective-permute-start(bf16[1024,512]{1,0:T(8,128)(2,1)S(1)} %pad_maximum_fusion.6), channel_id=1, source_target_pairs={{0,1},{1,0},{2,3},{3,2},{4,5},{5,4},{6,7},{7,6},{8,9},{9,8},{10,11... | collective-permute-start | bytes 3145736 | tf_op jit(solution)/shard_map/ppermute | solution.py:449
  262.2 2.2 copy-start.16
  262.3 2.7 copy-start.18
  262.3 3.2 %copy-start.26 = (bf16[256,512]{1,0:T(8,128)(2,1)S(1)}, bf16[256,512]{1,0:T(8,128)(2,1)}, u32[]{:S(2)}) copy-start(bf16[256,512]{1,0:T(8,128)(2,1)} %get-tuple-element.35) | copy-start | bytes 786436
  264.9 19.9 %collective-permute-start.21 = (bf16[3072,512]{1,0:T(8,128)(2,1)}, bf16[3072,512]{1,0:T(8,128)(2,1)}, u32[]{:S(2)}, u32[]{:S(2)}) collective-permute-start(bf16[3072,512]{1,0:T(8,128)(2,1)} %pad_maximum_fusion.1), channel_id=1, source_target_pairs={{0,1},{1,0},{2,3},{3,2},{4,5},{5,4},{6,7},{7,6},{8,9},{9,8},{10,11... | collective-permute-start | bytes 9437192 | tf_op jit(solution)/shard_map/ppermute | solution.py:449
  282.1 2.8 copy-start.17
  282.1 2.8 copy-start.19
  294.0 2.4 copy-start.1
  (2 other events, 1.4 us)
